TPU v7x, 32 devices: a whole 2x2x4 slice. The times are simulated.
32 devices in a mesh: chan: 8 (over z, y), win: 4 (over x, core).
Axes of the slice: x: 2, y: 2, z: 4, core: 2. Of those that a mesh axis runs over, the one named last changes fastest.
Arguments:
- samples: int32 [1536, 8, 6144], P('chan', 'win'), may hold values from -2048 to 2046
- exponents: int32 [1536, 8, 24], P('chan', 'win'), may hold values from 0 to 4
- alive: int32 [1536], P('chan'), may hold values 0 or 1
- offsets: int32 [32], P('chan'), may hold values from 0 to 191
Outputs:
- stacks: float32 [32, 384, 2048], P('chan', 'win')
All inputs are finite; a program needn't handle non-finite values. No bound on the sum of `alive` on one device may be relied on, other than what follows from the above.
Results may differ from a plain program's by a relative error of at most 0.0032.
Values may be sent and summed in bfloat16 or wider, within the bound.
A program may use at most 256 MiB of HBM per device.

v0:
```python
import math

import jax
import jax.numpy as jnp
from jax import lax
from jax.sharding import PartitionSpec as P

SEG = 1024
BAND = 192


def passed_along(block, axis, distance):
    devices = range(lax.axis_size(axis))
    route = [(i - distance, i) for i in devices if i - distance in devices]
    return lax.ppermute(block, axis, route)


def block_scale(exponents):
    levels = jnp.arange(5, dtype=jnp.int32)
    powers = jnp.exp2(levels.astype(jnp.float32))
    return jnp.sum(jnp.where(exponents[..., None] == levels, powers, 0.0), axis=-1)


def normalize(samples, exponents, alive):
    channels, windows, length = samples.shape
    block_count = exponents.shape[2]
    amplitude = samples.astype(jnp.float32).reshape(
        channels, windows, block_count, length // block_count
    )
    amplitude = amplitude * block_scale(exponents)[..., None]
    energy = jnp.mean(amplitude * amplitude, axis=(2, 3), keepdims=True)
    factor = alive.astype(jnp.float32)[:, None, None, None] * lax.rsqrt(energy + 1e-06)
    return (amplitude * factor).reshape(channels, windows, length).astype(jnp.bfloat16)


def forward_basis(seg_len):
    full_len = 2 * seg_len
    sample_index = jnp.arange(seg_len, dtype=jnp.int32)
    phases = sample_index[:, None] * sample_index[None, :] % full_len
    angles = phases.astype(jnp.float32) * (2.0 * math.pi / full_len)
    return jnp.concatenate([jnp.cos(angles), -jnp.sin(angles)], axis=1).astype(jnp.bfloat16)


def transform(normed, seg_len):
    channels, windows, length = normed.shape
    seg_count = length // seg_len
    segments = normed.reshape(channels * windows * seg_count, seg_len)
    spectra = jnp.dot(segments, forward_basis(seg_len), preferred_element_type=jnp.float32).astype(
        jnp.bfloat16
    )
    return spectra.reshape(channels, windows * seg_count, 2 * seg_len)


def inverse_table(seg_len, windows, seg_count):
    full_len = 2 * seg_len
    bin_index = jnp.arange(seg_len, dtype=jnp.int32)
    lag_index = jnp.arange(full_len, dtype=jnp.int32) - full_len // 2
    phases = bin_index[:, None] * lag_index[None, :] % full_len
    angles = phases.astype(jnp.float32) * (2.0 * math.pi / full_len)
    weight = jnp.where(bin_index == 0, 1.0, 2.0).astype(jnp.float32) / float(
        full_len * windows * seg_count * seg_len
    )
    return jnp.concatenate(
        [weight[:, None] * jnp.cos(angles), -weight[:, None] * jnp.sin(angles)], axis=0
    )


def widen(local_data):
    lower_parts = [passed_along(local_data, "chan", 1)]
    upper_parts = [passed_along(local_data, "chan", -1)]
    return jnp.concatenate(lower_parts + [local_data] + upper_parts, axis=0)


def shards(samples, exponents, alive, offsets):
    channels, windows, length = samples.shape
    bin_count = SEG
    normed = normalize(samples, exponents, alive)
    extended = widen(transform(normed, SEG))
    sources = jnp.take(extended, offsets + BAND, axis=0)

    def one_band(inputs):
        source, first_row = inputs
        band_rows = lax.dynamic_slice_in_dim(extended, first_row, 2 * BAND, 0)
        src_re = source[:, :bin_count]
        src_im = source[:, bin_count:]
        band_re = band_rows[..., :bin_count]
        band_im = band_rows[..., bin_count:]
        real_part = jnp.einsum("qk,rqk->rk", src_re, band_re, preferred_element_type=jnp.float32)
        real_part = real_part + jnp.einsum(
            "qk,rqk->rk", src_im, band_im, preferred_element_type=jnp.float32
        )
        imag_part = jnp.einsum("qk,rqk->rk", src_re, band_im, preferred_element_type=jnp.float32)
        imag_part = imag_part - jnp.einsum(
            "qk,rqk->rk", src_im, band_re, preferred_element_type=jnp.float32
        )
        return jnp.concatenate([real_part, imag_part], axis=-1)

    cross_terms = lax.map(one_band, (sources, offsets))
    stacked = lax.psum_scatter(cross_terms, "win", scatter_dimension=1, tiled=True)
    lag_table = inverse_table(SEG, windows * lax.axis_size("win"), length // SEG)
    src_count, recv_count, spec_width = stacked.shape
    result = jnp.dot(
        stacked.reshape(src_count * recv_count, spec_width),
        lag_table,
        precision=lax.Precision.HIGHEST,
        preferred_element_type=jnp.float32,
    )
    return result.reshape(src_count, recv_count, 2 * SEG)


def solution(mesh):
    placed = (P("chan", "win", None), P("chan", "win", None), P("chan"), P("chan"))
    return jax.shard_map(
        shards, mesh=mesh, in_specs=placed, out_specs=P("chan", "win", None), check_vma=False
    )
```

profile of v0, /device:TPU:0, one launch (start us, length us, event | category | flops | bytes accessed | tf_op | source)
XLA Modules:
  0.0 830.4 jit_solution(14464679196925269945)
XLA Ops:
  6.5 17.7 %negate_convert_fusion = (bf16[1024,1024]{1,0:T(8,128)(2,1)S(1)}, bf16[1024,1024]{1,0:T(8,128)(2,1)}) fusion(), kind=kLoop, calls=%fused_computation.50 | loop fusion | flops 17825792 | bytes 4194304 | tf_op jit(solution)/shard_map/convert.1
  24.3 0.9 select_reduce_fusion
  25.3 4.3 mul.108
  29.6 12.3 %mul.109 = f32[192,2,6144]{2,1,0:T(2,128)} reshape(f32[192,2,24,256]{3,2,1,0:T(8,128)} %mul.108) | data formatting | bytes 18874368 | tf_op jit(solution)/shard_map/mul | solution.py:30
  41.8 8.8 %multiply_reduce_fusion = f32[192,2]{1,0:T(8,128)S(1)} fusion(f32[192,2,6144]{2,1,0:T(2,128)} %mul.109, s32[192,2,6144]{2,1,0:T(2,128)} %param.6), kind=kLoop, calls=%fused_computation.31 | loop fusion | flops 9436800 | bytes 18875904 | tf_op jit(solution)/shard_map/reduce_sum | solution.py:31
  50.9 9.9 %multiply_convert_fusion = bf16[192,2,6144]{2,1,0:T(2,128)(2,1)} fusion(f32[192,2]{1,0:T(8,128)S(1)} %copy.25, f32[192,2,6144]{2,1,0:T(2,128)} %mul.109, s32[192,2,6144]{2,1,0:T(2,128)} %param.6), kind=kLoop, calls=%fused_computation.30 | loop fusion | flops 9437184 | bytes 23594496 | tf_op jit(solution)/shard_map/convert_element_type | solution.py:33
  60.8 11.2 %reshape.62 = bf16[2304,1024]{1,0:T(8,128)(2,1)} reshape(bf16[192,2,6144]{2,1,0:T(2,128)(2,1)} %multiply_convert_fusion) | data formatting | bytes 9437184 | tf_op jit(solution)/shard_map/reshape | solution.py:47
  72.0 14.6 %convolution_convert_fusion = bf16[2304,2048]{1,0:T(8,128)(2,1)} fusion(bf16[2304,1024]{1,0:T(8,128)(2,1)} %reshape.62, bf16[1024,1024]{1,0:T(8,128)(2,1)S(1)} %get-tuple-element.57, bf16[1024,1024]{1,0:T(8,128)(2,1)} %get-tuple-element.58), kind=kOutput, calls=%fused_computation.29 | convolution fusion | flops 9676783616 | bytes 18350080 | tf_op jit(solution)/shard_map/dot_general | solution.py:48
  86.6 15.1 %reshape.63 = bf16[192,12,2048]{2,1,0:T(8,128)(2,1)} reshape(bf16[2304,2048]{1,0:T(8,128)(2,1)} %convolution_convert_fusion) | data formatting | bytes 18874368 | tf_op jit(solution)/shard_map/reshape | solution.py:51
  101.8 13.4 %copy.26 = bf16[192,12,2048]{2,0,1:T(8,128)(2,1)} copy(bf16[192,12,2048]{2,1,0:T(8,128)(2,1)} %reshape.63) | data formatting | bytes 18874368 | tf_op jit(solution)/shard_map/reshape | solution.py:51
  115.2 8.5 %collective-permute-start = (bf16[192,12,2048]{2,0,1:T(8,128)(2,1)}, bf16[192,12,2048]{2,0,1:T(8,128)(2,1)}, u32[]{:S(2)}, u32[]{:S(2)}) collective-permute-start(bf16[192,12,2048]{2,0,1:T(8,128)(2,1)} %copy.26), channel_id=1, source_target_pairs={{0,4},{4,8},{8,12},{12,16},{16,20},{20,24},{24,28},{1,5},{5,9},{9,... | collective-permute-start | bytes 28311560 | tf_op jit(solution)/shard_map/ppermute | solution.py:15
  123.7 1.3 collective-permute-start.1
  125.0 399.8 %collective-permute-done = bf16[192,12,2048]{2,0,1:T(8,128)(2,1)} collective-permute-done((bf16[192,12,2048]{2,0,1:T(8,128)(2,1)}, bf16[192,12,2048]{2,0,1:T(8,128)(2,1)}, u32[]{:S(2)}, u32[]{:S(2)}) %collective-permute-start) | collective-permute-done | bytes 9437216 | tf_op jit(solution)/shard_map/ppermute | solution.py:15
  524.8 12.9 %copy_dynamic-update-slice_fusion.1 = bf16[576,12,2048]{2,1,0:T(8,128)(2,1)} fusion(bf16[192,12,2048]{2,0,1:T(8,128)(2,1)} %collective-permute-done), kind=kLoop, calls=%fused_computation.25 | loop fusion | bytes 22020096
  537.7 5.1 constant_dynamic-update-slice_fusion
  542.8 12.9 %copy_dynamic-update-slice_fusion = bf16[576,12,2048]{2,1,0:T(8,128)(2,1)} fusion(bf16[576,12,2048]{2,1,0:T(8,128)(2,1)} %constant_dynamic-update-slice_fusion, bf16[192,12,2048]{2,0,1:T(8,128)(2,1)} %collective-permute-done.1), kind=kLoop, calls=%fused_computation.24 | loop fusion | bytes 22020096 | tf_op jit(solution)/shard_map/concatenate | solution.py:71
  555.6 1.5 gather_fusion
  557.2 140.8 %while.10 = (s32[]{:T(128)}, f32[4,384,2048]{2,1,0:T(8,128)}, s32[4]{0:T(128)S(1)}, bf16[576,12,2048]{2,1,0:T(8,128)(2,1)}, bf16[4,12,2048]{2,1,0:T(8,128)(2,1)S(1)}, /*index=5*/s32[]{:T(128)}, s32[]{:T(128)}, s32[]{:T(128)}, s32[]{}) while((s32[]{:T(128)}, f32[4,384,2048]{2,1,0:T(8,128)}, s32[4]{0:T(128)S(1)}, ...), condition=%wide.region_3.4_spmd, body=%wide.region_2.3_spmd.sunk | while | flops 47210500 | bytes 41239200 | solution.py:98
  559.7 30.0 %fusion.34 = (f32[1024,384]{0,1:T(8,128)S(1)}, f32[1024,384]{0,1:T(8,128)S(1)}, f32[1024,384]{0,1:T(8,128)S(1)}, f32[1024,384]{0,1:T(8,128)S(1)}) fusion(f32[1024,12]{0,1:T(8,128)S(1)} %get-tuple-element.100, bf16[576,12,2048]{2,1,0:T(8,128)(2,1)} %get-tuple-element.129, s32[]{:T(128)S(6)} %select_n.78, s32[]{:T(128)S(6)} %add.101, ...), kind=kLoop, calls=%fused_computation.7.clone.1 | loop fusion | flops 45613056 | bytes 25264136 | tf_op jit(solution)/shard_map/while/body/eval_jaxpr/qk,rqk->rk/dot_general | solution.py:89
  589.7 0.7 subtract_bitcast_fusion.2
  590.4 2.0 fusion.35
  594.9 30.0 %fusion.34 = (f32[1024,384]{0,1:T(8,128)S(1)}, f32[1024,384]{0,1:T(8,128)S(1)}, f32[1024,384]{0,1:T(8,128)S(1)}, f32[1024,384]{0,1:T(8,128)S(1)}) fusion(f32[1024,12]{0,1:T(8,128)S(1)} %get-tuple-element.100, bf16[576,12,2048]{2,1,0:T(8,128)(2,1)} %get-tuple-element.129, s32[]{:T(128)S(6)} %select_n.78, s32[]{:T(128)S(6)} %add.101, ...), kind=kLoop, calls=%fused_computation.7.clone.1 | loop fusion | flops 45613056 | bytes 25264136 | tf_op jit(solution)/shard_map/while/body/eval_jaxpr/qk,rqk->rk/dot_general | solution.py:89
  624.9 0.7 subtract_bitcast_fusion.2
  625.6 2.0 fusion.35
  630.1 30.0 %fusion.34 = (f32[1024,384]{0,1:T(8,128)S(1)}, f32[1024,384]{0,1:T(8,128)S(1)}, f32[1024,384]{0,1:T(8,128)S(1)}, f32[1024,384]{0,1:T(8,128)S(1)}) fusion(f32[1024,12]{0,1:T(8,128)S(1)} %get-tuple-element.100, bf16[576,12,2048]{2,1,0:T(8,128)(2,1)} %get-tuple-element.129, s32[]{:T(128)S(6)} %select_n.78, s32[]{:T(128)S(6)} %add.101, ...), kind=kLoop, calls=%fused_computation.7.clone.1 | loop fusion | flops 45613056 | bytes 25264136 | tf_op jit(solution)/shard_map/while/body/eval_jaxpr/qk,rqk->rk/dot_general | solution.py:89
  660.1 0.7 subtract_bitcast_fusion.2
  660.8 2.1 fusion.35
  665.3 30.0 %fusion.34 = (f32[1024,384]{0,1:T(8,128)S(1)}, f32[1024,384]{0,1:T(8,128)S(1)}, f32[1024,384]{0,1:T(8,128)S(1)}, f32[1024,384]{0,1:T(8,128)S(1)}) fusion(f32[1024,12]{0,1:T(8,128)S(1)} %get-tuple-element.100, bf16[576,12,2048]{2,1,0:T(8,128)(2,1)} %get-tuple-element.129, s32[]{:T(128)S(6)} %select_n.78, s32[]{:T(128)S(6)} %add.101, ...), kind=kLoop, calls=%fused_computation.7.clone.1 | loop fusion | flops 45613056 | bytes 25264136 | tf_op jit(solution)/shard_map/while/body/eval_jaxpr/qk,rqk->rk/dot_general | solution.py:89
  696.0 2.0 fusion.35
  698.1 34.7 %cosine_multiply_fusion = (f32[1024,2048]{1,0:T(8,128)}, f32[1024,2048]{1,0:T(8,128)}) fusion(s32[2048]{0:T(1024)S(1)} %iota_add_fusion, f32[1024]{0:T(1024)S(1)} %get-tuple-element.59, f32[1024]{0:T(1024)S(1)} %get-tuple-element.60), kind=kLoop, calls=%fused_computation.37 | loop fusion | flops 33554432 | bytes 16793600 | tf_op jit(solution)/shard_map/mul | solution.py:64
  732.7 65.7 %reduce-scatter.2.cloned.1.call-done = f32[4,96,2048]{2,1,0:T(8,128)} async-done(((f32[4,384,2048]{2,1,0:T(8,128)}), f32[4,96,2048]{2,1,0:T(8,128)}) %reduce-scatter.2.cloned.1.call-update) | async-done | bytes 3145744 | tf_op jit(solution)/shard_map/reduce_scatter | solution.py:99
  798.4 25.1 %fusion.7 = f32[4,96,2048]{2,1,0:T(8,128)} fusion(f32[4,96,2048]{2,1,0:T(8,128)} %reduce-scatter.2.cloned.1.call-done, f32[1024,2048]{1,0:T(8,128)} %get-tuple-element.56, f32[1024,2048]{1,0:T(8,128)} %get-tuple-element.55), kind=kOutput, calls=%fused_computation.21 | convolution fusion | flops 19331547136 | bytes 23068672 | tf_op jit(solution)/shard_map/dot_general | solution.py:102
  (34 shorter events, 3.7 us)
Async XLA Ops:
  6.5 791.9 %reduce-scatter.2.cloned.1.call-start = ((), (), s32[]{:S(2)}) async-start(), calls=%async_computation.1 | async-start | bytes 15728640 | tf_op jit(solution)/shard_map/reduce_scatter | solution.py:99
  41.8 8.9 %copy-start.1 = (s32[192]{0:T(256)S(1)}, s32[192]{0:T(256)}, u32[]{:S(2)}) copy-start(s32[192]{0:T(256)} %param.8) | copy-start | bytes 2308
  101.8 23.2 %copy-start.2 = (s32[4]{0:T(128)S(1)}, s32[4]{0:T(128)}, u32[]{:S(2)}) copy-start(s32[4]{0:T(128)} %param.9) | copy-start | bytes 52
  115.2 409.6 %collective-permute-start = (bf16[192,12,2048]{2,0,1:T(8,128)(2,1)}, bf16[192,12,2048]{2,0,1:T(8,128)(2,1)}, u32[]{:S(2)}, u32[]{:S(2)}) collective-permute-start(bf16[192,12,2048]{2,0,1:T(8,128)(2,1)} %copy.26), channel_id=1, source_target_pairs={{0,4},{4,8},{8,12},{12,16},{16,20},{20,24},{24,28},{1,5},{5,9},{9,... | collective-permute-start | bytes 28311560 | tf_op jit(solution)/shard_map/ppermute | solution.py:15
  123.7 419.1 %collective-permute-start.1 = (bf16[192,12,2048]{2,0,1:T(8,128)(2,1)}, bf16[192,12,2048]{2,0,1:T(8,128)(2,1)}, u32[]{:S(2)}, u32[]{:S(2)}) collective-permute-start(bf16[192,12,2048]{2,0,1:T(8,128)(2,1)} %copy.26), channel_id=1, source_target_pairs={{4,0},{8,4},{12,8},{16,12},{20,16},{24,20},{28,24},{5,1},{9,5},{13... | collective-permute-start | bytes 28311560 | tf_op jit(solution)/shard_map/ppermute | solution.py:15
  125.0 412.7 %copy-start = (bf16[192,12,2048]{2,1,0:T(8,128)(2,1)S(1)}, bf16[192,12,2048]{2,1,0:T(8,128)(2,1)}, u32[]{:S(2)}) copy-start(bf16[192,12,2048]{2,1,0:T(8,128)(2,1)} %reshape.63) | copy-start | bytes 28311556
Sparse Core Ops, SparseCore 0:
  698.2 100.2 reduce-scatter.1
where the time goes:
time: 832 us; the launch traced here: 830 us
  waiting for transfers between devices  465 us (56%)
  other arithmetic  203 us (24%)
  local copies, waits for them, and re-layouts  91.5 us (11%)
  matrix products  39.7 us (5%)
  between operations  13.5 us (2%)
  starting transfers between devices  9.76 us (1%)
    ppermute x2, waiting for transfers between devices, passed_along(): return lax.ppermute(block, axis, route)  400 us
    dot_general x4, other arithmetic, one_band(): jnp.einsum('qk,rqk->rk', src_im, band_im, preferred_element_type=jnp.floa...  120 us
    reduce_scatter x1, waiting for transfers between devices, shards(): lax.psum_scatter(cross_terms, 'win', scatter_dimension=1, tiled=True)  65.7 us
    mul x1, other arithmetic, inverse_table(): weight[:, None] * jnp.cos(angles)  34.7 us
    reshape x2, local copies, waits for them, and re-layouts, transform(): return spectra.reshape(channels, windows * seg_count, 2 * seg_len)  28.5 us
    dot_general x1, matrix products, shards(): jnp.dot(stacked.reshape(src_count * recv_count, spec_width), lag_table, p...  25.1 us
    unnamed x8, local copies, waits for them, and re-layouts  18 us
    another operation x1, other arithmetic  17.7 us
  transfers between devices with their start and end apart: 3, of which 2 were waited for; matrix products, arithmetic and copies ran while one was open for 6% of the time, Pallas kernels for 0%

commit v1 on v0

v1 whole, which is shorter than its diff:
```python
import functools

import jax
import jax.numpy as jnp
import ml_dtypes
import numpy as np
from jax import lax
from jax.experimental import pallas as pl
from jax.experimental.pallas import tpu as pltpu
from jax.sharding import PartitionSpec as P

SEG = 1024
SCALE_LEN = 256
GROUP = 16
F32, BF16 = jnp.float32, jnp.bfloat16


def bin_order():
    bins = np.arange(SEG).reshape(-1, 1, GROUP)
    return np.concatenate([bins, bins + SEG], axis=1).reshape(-1)


@functools.lru_cache(None)
def forward_basis():
    i = np.arange(SEG)
    angles = (i[:, None] * i[None, :] % (2 * SEG)) * (2.0 * np.pi / (2 * SEG))
    basis = np.concatenate([np.cos(angles), -np.sin(angles)], axis=1)
    return basis.astype(np.float32).astype(ml_dtypes.bfloat16)


@functools.lru_cache(None)
def lag_tables(windows, seg_count):
    full = 2 * SEG
    k = np.arange(SEG)
    lag = np.arange(full) - SEG
    angles = (k[:, None] * lag[None, :] % full) * (2.0 * np.pi / full)
    weight = np.where(k == 0, 1.0, 2.0)[:, None] / float(full * windows * seg_count * SEG)
    table = np.concatenate([weight * np.cos(angles), -weight * np.sin(angles)], axis=0)
    table = table[bin_order()].astype(np.float32)
    high = table.astype(ml_dtypes.bfloat16)
    low = (table - high.astype(np.float32)).astype(ml_dtypes.bfloat16)
    return high, low


def norm_kernel(samples, exponents, alive, out, raw, sems):
    windows, channels, length = raw.shape
    copies = [
        pltpu.make_async_copy(samples.at[:, w, :], raw.at[w], sems.at[w]) for w in range(windows)
    ]
    for copy in copies:
        copy.start()
    for w in range(windows):
        copies[w].wait()
        scale = jnp.left_shift(1, exponents[w]).astype(F32)
        total = jnp.zeros((channels, SCALE_LEN), F32)
        for b in range(length // SCALE_LEN):
            x = raw[w, :, b * SCALE_LEN : (b + 1) * SCALE_LEN].astype(F32) * scale[:, b : b + 1]
            total = total + x * x
        energy = jnp.sum(total, axis=1, keepdims=True) / length
        factor = alive[...] * lax.rsqrt(energy + 1e-06)
        for b in range(length // SCALE_LEN):
            x = raw[w, :, b * SCALE_LEN : (b + 1) * SCALE_LEN].astype(F32) * scale[:, b : b + 1]
            n, part = divmod(b * SCALE_LEN, SEG)
            out[w * (length // SEG) + n, part : part + SCALE_LEN, :] = (x * factor).T.astype(BF16)


def normalize_blocks(samples, exponents, alive):
    channels, windows, length = samples.shape
    return pl.pallas_call(
        norm_kernel,
        out_shape=jax.ShapeDtypeStruct((windows * length // SEG, SEG, channels), BF16),
        in_specs=[
            pl.BlockSpec(memory_space=pl.ANY),
            pl.BlockSpec(memory_space=pltpu.VMEM),
            pl.BlockSpec(memory_space=pltpu.VMEM),
        ],
        out_specs=pl.BlockSpec(memory_space=pltpu.VMEM),
        scratch_shapes=[
            pltpu.VMEM((windows, channels, length), jnp.int32),
            pltpu.SemaphoreType.DMA((windows,)),
        ],
        compiler_params=pltpu.CompilerParams(vmem_limit_bytes=48 * 2**20),
    )(samples, jnp.swapaxes(exponents, 0, 1), alive.astype(F32)[:, None])


def cross_kernel(offsets, basis, blocks, rows, out, spec, weights, cross):
    seg_count, _, channels = blocks.shape
    groups, terms, depth = rows.shape
    sources = terms // 2
    for n in range(seg_count):
        part = jnp.dot(basis[...], blocks[n], preferred_element_type=F32).astype(BF16)
        for q in range(groups):
            spec[q, n * 2 * GROUP : (n + 1) * 2 * GROUP, :] = part[q * 2 * GROUP : (q + 1) * 2 * GROUP]
    lane_bin = lax.broadcasted_iota(jnp.int32, (GROUP, depth), 1) % GROUP
    same = lane_bin == lax.broadcasted_iota(jnp.int32, (GROUP, depth), 0)
    for q in range(groups):
        for s in range(terms):
            row = jnp.broadcast_to(rows[q, s : s + 1, :], (GROUP, depth))
            weights[q % 2, s * GROUP : (s + 1) * GROUP, :] = jnp.where(same, row, 0.0).astype(BF16)
        product = jnp.dot(weights[q % 2], spec[q], preferred_element_type=F32).astype(BF16)
        for s in range(sources):
            cross[s, q * 2 * GROUP : (q + 1) * 2 * GROUP, :] = product[s * 2 * GROUP : (s + 1) * 2 * GROUP]
    target = lax.broadcasted_iota(jnp.int32, (channels, channels), 0)
    origin = lax.broadcasted_iota(jnp.int32, (channels, channels), 1)
    half = channels // 2
    for s in range(sources):
        at = target + offsets[s]
        at = jnp.where(at >= channels, at - channels, at)
        turn = jnp.where(at == origin, 1.0, 0.0).astype(BF16)
        turned = lax.dot_general(
            turn, cross[s], (((1,), (1,)), ((), ())), preferred_element_type=F32
        ).astype(BF16)
        out[0, s] = turned[:half]
        out[1, s] = turned[half:]


def cross_terms(offsets, blocks, rows, first, count):
    seg_count, _, channels = blocks.shape
    _, terms, depth = rows.shape
    step = 8
    width = step * 2 * GROUP
    basis = jnp.asarray(forward_basis().T[bin_order()][first * 2 * GROUP : (first + count) * 2 * GROUP])
    return pl.pallas_call(
        cross_kernel,
        grid_spec=pltpu.PrefetchScalarGridSpec(
            num_scalar_prefetch=1,
            grid=(count // step,),
            in_specs=[
                pl.BlockSpec((width, SEG), lambda i, o: (i, 0)),
                pl.BlockSpec((seg_count, SEG, channels), lambda i, o: (0, 0, 0)),
                pl.BlockSpec((step, terms, depth), lambda i, o: (i + first // step, 0, 0)),
            ],
            out_specs=pl.BlockSpec((2, terms // 2, channels // 2, width), lambda i, o: (0, 0, 0, i)),
            scratch_shapes=[
                pltpu.VMEM((step, depth, channels), BF16),
                pltpu.VMEM((2, terms * GROUP, depth), BF16),
                pltpu.VMEM((terms // 2, width, channels), BF16),
            ],
        ),
        out_shape=jax.ShapeDtypeStruct((2, terms // 2, channels // 2, count * 2 * GROUP), BF16),
        compiler_params=pltpu.CompilerParams(vmem_limit_bytes=48 * 2**20),
    )(offsets, basis, blocks, rows)


def lag_kernel(kept, came, high, low, out):
    total = kept[...].astype(F32) + came[...].astype(F32)
    top = total.astype(BF16)
    rest = (total - top.astype(F32)).astype(BF16)
    result = jnp.dot(top, low[...], preferred_element_type=F32)
    result = result + jnp.dot(rest, high[...], preferred_element_type=F32)
    out[...] = result + jnp.dot(top, high[...], preferred_element_type=F32)


def lag_product(kept, came, high, low):
    rows, depth = kept.shape
    width = 512
    return pl.pallas_call(
        lag_kernel,
        grid=(2 * SEG // width,),
        in_specs=[
            pl.BlockSpec((rows, depth), lambda i: (0, 0)),
            pl.BlockSpec((rows, depth), lambda i: (0, 0)),
            pl.BlockSpec((depth, width), lambda i: (0, i)),
            pl.BlockSpec((depth, width), lambda i: (0, i)),
        ],
        out_specs=pl.BlockSpec((rows, width), lambda i: (0, i)),
        out_shape=jax.ShapeDtypeStruct((rows, 2 * SEG), F32),
        compiler_params=pltpu.CompilerParams(vmem_limit_bytes=48 * 2**20),
    )(kept, came, high, low)


def passed_along(block, axis, distance):
    devices = range(lax.axis_size(axis))
    route = [(i - distance, i) for i in devices if i - distance in devices]
    return lax.ppermute(block, axis, route)


def swapped(block, bit):
    return lax.ppermute(block, "win", [(i, i ^ bit) for i in range(lax.axis_size("win"))])


def source_rows(samples, exponents, alive, offsets):
    picked = [
        [lax.dynamic_slice_in_dim(a, offsets[j], 1, 0) for j in range(offsets.shape[0])]
        for a in (samples, exponents, alive)
    ]
    samples, exponents, alive = (jnp.concatenate(p, axis=0) for p in picked)
    count, windows, length = samples.shape
    scale = jnp.left_shift(1, exponents).astype(F32)
    amplitude = samples.astype(F32).reshape(count, windows, -1, SCALE_LEN) * scale[..., None]
    energy = jnp.mean(amplitude * amplitude, axis=(2, 3), keepdims=True)
    factor = alive.astype(F32)[:, None, None, None] * lax.rsqrt(energy + 1e-06)
    normed = (amplitude * factor).astype(BF16).reshape(count, windows * length)
    tail = jnp.broadcast_to(offsets.astype(BF16)[:, None], (count, 128))
    return jnp.concatenate([normed, tail], axis=1)


def source_terms(sources):
    count, length = sources.shape
    seg_count = length // SEG
    spectra = jnp.dot(
        sources.reshape(count * seg_count, SEG), jnp.asarray(forward_basis()), preferred_element_type=F32
    ).astype(BF16)
    spectra = spectra.reshape(count, seg_count, 2, SEG // GROUP, GROUP)
    real, imag = spectra[:, :, 0], spectra[:, :, 1]
    pair = jnp.stack([jnp.stack([real, imag], 2), jnp.stack([-imag, real], 2)], 1)
    rows = jnp.transpose(pair, (4, 0, 1, 2, 3, 5))
    return rows.reshape(SEG // GROUP, count * 2, seg_count * 2 * GROUP).astype(F32)


CHUNKS = 1


def shards(samples, exponents, alive, offsets):
    channels, windows, length = samples.shape
    per_device = offsets.shape[0]
    win = lax.axis_index("win")
    core, side = win % 2, win // 2
    own = source_rows(samples, exponents, alive, offsets)
    sources = jnp.concatenate(
        [passed_along(own, "chan", 1), own, passed_along(own, "chan", -1)], axis=0
    )
    places = sources[:, windows * length].astype(jnp.int32)
    rows = source_terms(sources[:, : windows * length])
    blocks = normalize_blocks(samples, exponents, alive)
    half = channels // 2
    turned = (core * half + jnp.arange(half, dtype=jnp.int32))[None, :, None]
    low_part = turned < (channels - offsets)[:, None, None]
    kept, came = [], []
    groups = SEG // GROUP
    count = groups // CHUNKS
    for c in range(CHUNKS):
        terms = cross_terms(places, blocks, rows, c * count, count)
        mine = lax.dynamic_index_in_dim(terms, core, 0, keepdims=False)
        other = swapped(lax.dynamic_index_in_dim(terms, 1 - core, 0, keepdims=False), 1)
        pair = (mine.astype(F32) + other.astype(F32)).astype(BF16)
        below = passed_along(pair[2 * per_device :], "chan", 1)
        above = passed_along(pair[:per_device], "chan", -1)
        here = pair[per_device : 2 * per_device]
        first = jnp.where(low_part, below, here)
        second = jnp.where(low_part, here, above)
        kept.append(jnp.where(side == 0, first, second))
        came.append(swapped(jnp.where(side == 0, second, first), 2))
    kept = jnp.concatenate(kept, axis=-1).reshape(per_device * half, 2 * SEG)
    came = jnp.concatenate(came, axis=-1).reshape(per_device * half, 2 * SEG)
    high, low = lag_tables(windows * lax.axis_size("win"), length // SEG)
    result = lag_product(kept, came, jnp.asarray(high), jnp.asarray(low))
    return result.reshape(per_device, half, 2 * SEG)


def solution(mesh):
    placed = (P("chan", "win", None), P("chan", "win", None), P("chan"), P("chan"))
    return jax.shard_map(
        shards, mesh=mesh, in_specs=placed, out_specs=P("chan", "win", None), check_vma=False
    )
```

time: 832 us -> 248 us (0.30)
  waiting for transfers between devices: 465 us -> 109 us
  other arithmetic: 203 us -> 16.6 us
  Pallas kernels: 0 us -> 53 us
  local copies, waits for them, and re-layouts: 91.5 us -> 41.6 us
  matrix products: 39.7 us -> 2.98 us
    ppermute x2 -> x4, waiting for transfers between devices: 400 us -> 65.6 us  [passed_along(): return lax.ppermute(block, axis, route)]
    dot_general x4 -> x0, other arithmetic: 120 us -> none  [one_band(): jnp.einsum('qk,rqk->rk', src_im, band_im, preferred_element_type=jnp.floa...]
    reduce_scatter x1 -> x0, waiting for transfers between devices: 65.7 us -> none  [shards(): lax.psum_scatter(cross_terms, 'win', scatter_dimension=1, tiled=True)]
    pallas_call x0 -> x3, Pallas kernels: none -> 53 us  [the longest x1 30.2 us: cross_terms(): pl.pallas_call(cross_kernel, grid_spec=pltpu.PrefetchScalarGridSpec(num_s...]
    ppermute x0 -> x2, waiting for transfers between devices: none -> 43.1 us  [swapped(): lax.ppermute(block, 'win', [(i, i ^ bit) for i in range(lax.axis_size('wi...]
    dot_general x2 -> x1, matrix products: 39.7 us -> 2.98 us  [source_terms(): jnp.dot(sources.reshape(count * seg_count, SEG), jnp.asarray(forward_basi...]
    mul x2 -> x1, other arithmetic: 34.7 us -> 0.07 us  [source_rows(): factor = alive.astype(F32)[:, None, None, None] * lax.rsqrt(energy + 1e-06)]
    reshape x3 -> x2, local copies, waits for them, and re-layouts: 39.8 us -> 5.75 us  [the longest x1 5.29 us: source_terms(): spectra = spectra.reshape(count, seg_count, 2, SEG // GROUP, GROUP)]
  transfers between devices with their start and end apart: 3 -> 6, of which waited for: 2 -> 4; matrix products, arithmetic and copies ran while one was open for 6% -> 0% of each run, Pallas kernels for 0% -> 4%
where the time goes in v1:
time: 248 us; the launch traced here: 247 us
  waiting for transfers between devices  109 us (44%)
  Pallas kernels  53 us (21%)
  local copies, waits for them, and re-layouts  41.6 us (17%)
  other arithmetic  16.6 us (7%)
  starting transfers between devices  16.3 us (7%)
  between operations  7.71 us (3%)
  matrix products  2.98 us (1%)
    ppermute x4, waiting for transfers between devices, passed_along(): return lax.ppermute(block, axis, route)  65.6 us
    ppermute x2, waiting for transfers between devices, swapped(): lax.ppermute(block, 'win', [(i, i ^ bit) for i in range(lax.axis_size('wi...  43.1 us
    pallas_call x1, Pallas kernels, cross_terms(): pl.pallas_call(cross_kernel, grid_spec=pltpu.PrefetchScalarGridSpec(num_s...  30.2 us
    ppermute x4, starting transfers between devices, passed_along(): return lax.ppermute(block, axis, route)  14.7 us
    pallas_call x1, Pallas kernels, lag_product(): pl.pallas_call(lag_kernel, grid=(2 * SEG // width,), in_specs=[pl.BlockSp...  13.6 us
    pallas_call x1, Pallas kernels, normalize_blocks(): pl.pallas_call(norm_kernel, out_shape=jax.ShapeDtypeStruct((windows * len...  9.23 us
    another operation x2, local copies, waits for them, and re-layouts, source_terms(): jnp.stack([jnp.stack([real, imag], 2), jnp.stack([-imag, real], 2)], 1)  8.88 us
    slice x2, local copies, waits for them, and re-layouts, source_terms(): real, imag = (spectra[:, :, 0], spectra[:, :, 1])  7.06 us
  transfers between devices with their start and end apart: 6, of which 4 were waited for; matrix products, arithmetic and copies ran while one was open for 0% of the time, Pallas kernels for 4%

profile of v1, /device:TPU:0, one launch (start us, length us, event | category | flops | bytes accessed | tf_op | source)
XLA Modules:
  0.0 246.8 jit_solution(16909214101842876451)
XLA Ops:
  0.7 1.4 fusion.11
  7.1 0.9 copy.35
  10.5 1.5 fusion.10
  12.0 0.9 constant_dynamic-slice_fusion.7
  13.4 2.5 %add_convert_fusion.2 = f32[4]{0:T(128)S(1)} fusion(s32[1]{0:T(128)} %get-tuple-element.22, s32[1]{0:T(128)} %get-tuple-element.20, s32[1]{0:T(128)} %get-tuple-element.21, s32[1]{0:T(128)} %get-tuple-element.19), kind=kLoop, calls=%fused_computation.39 | loop fusion | flops 16 | bytes 32 | tf_op jit(solution)/shard_map/convert_element_type | solution.py:192
  16.8 1.3 collective-permute-start.1
  18.1 5.5 %collective-permute-start = (bf16[4,12416]{1,0:T(4,128)(2,1)S(1)}, bf16[4,12416]{1,0:T(4,128)(2,1)S(1)}, u32[]{:S(2)}, u32[]{:S(2)}) collective-permute-start(bf16[4,12416]{1,0:T(4,128)(2,1)S(1)} %pad_maximum_fusion.3), channel_id=1, source_target_pairs={{0,4},{4,8},{8,12},{12,16},{16,20},{20,24},{24,28},{1,5},{5,9},{9,... | collective-permute-start | bytes 297992 | tf_op jit(solution)/shard_map/ppermute | solution.py:175
  23.8 9.2 %shard_map.82.blocks = bf16[12,1024,192]{2,1,0:T(8,128)(2,1)} custom-call(s32[192,2,6144]{2,1,0:T(2,128)} %samples.1, s32[2,192,24]{2,1,0:T(8,128)S(1)} %bitcast.59, f32[192,1]{1,0:T(8,128)S(1)} %copy.41.alive), custom_call_target="tpu_custom_call" | custom-call | tf_op jit(solution)/shard_map/pallas_call | solution.py:69
  33.7 3.0 %convolution_convert_fusion = bf16[144,2048]{1,0:T(8,128)(2,1)S(1)} fusion(bf16[144,1024]{1,0:T(8,128)(2,1)S(1)} %reshape.162, bf16[1024,2048]{1,0:T(8,128)(2,1)} %constant.59.clone), kind=kOutput, calls=%fused_computation.3 | convolution fusion | flops 604274688 | bytes 5079040 | tf_op jit(solution)/shard_map/dot_general | solution.py:201
  36.7 5.3 %reshape.163 = bf16[12,12,2,64,16]{4,3,2,1,0:T(8,128)(2,1)} reshape(bf16[144,2048]{1,0:T(8,128)(2,1)S(1)} %convolution_convert_fusion) | data formatting | bytes 1179648 | tf_op jit(solution)/shard_map/reshape | solution.py:204
  42.0 5.0 %stack.14 = bf16[12,1,12,2,64,16]{5,4,3,2,0,1:T(8,128)(2,1)} reshape(bf16[144,2048]{1,0:T(8,128)(2,1)S(1)} %convolution_convert_fusion) | data formatting | bytes 1179648 | tf_op jit(solution)/shard_map/stack | solution.py:206
  47.0 5.4 %fusion.9 = (bf16[12,12,1,64,16]{4,3,2,1,0:T(8,128)(2,1)}, bf16[12,12,1,64,16]{4,3,2,1,0:T(8,128)(2,1)S(1)}) fusion(bf16[12,12,2,64,16]{4,3,2,1,0:T(8,128)(2,1)} %reshape.163), kind=kLoop, calls=%fused_computation.43 | loop fusion | bytes 1179648 | tf_op jit(solution)/shard_map/slice | solution.py:205
  52.4 2.7 %copy.47 = bf16[12,12,1,64,16]{3,4,2,1,0:T(8,128)(2,1)} copy(bf16[12,12,1,64,16]{4,3,2,1,0:T(8,128)(2,1)} %get-tuple-element.13) | data formatting | bytes 589824
  55.1 1.2 neg.4
  56.3 1.6 copy.43
  58.0 3.9 %copy.44 = bf16[12,1,12,2,64,16]{4,5,3,2,1,0:T(8,128)(2,1)S(1)} copy(bf16[12,1,12,2,64,16]{5,4,3,2,0,1:T(8,128)(2,1)} %stack.14) | data formatting | bytes 1179648 | tf_op jit(solution)/shard_map/stack | solution.py:206
  62.1 2.8 %maximum_convert_fusion = f32[12,2,12,2,64,16]{4,5,3,2,1,0:T(8,128)} fusion(bf16[12,1,12,2,64,16]{4,5,3,2,1,0:T(8,128)(2,1)S(1)} %maximum_bitcast_fusion, bf16[12,1,12,2,64,16]{4,5,3,2,1,0:T(8,128)(2,1)S(1)} %copy.44), kind=kLoop, calls=%fused_computation.4 | loop fusion | flops 1179648 | bytes 3538944 | tf_op jit(solution)/shard_map/convert_element_type | solution.py:208
  64.9 3.9 %copy.46.rows = f32[64,24,384]{2,1,0:T(8,128)S(1)} copy(f32[64,24,384]{0,2,1:T(8,128)} %bitcast.60) | data formatting | bytes 4718592 | tf_op jit(solution)/shard_map/convert_element_type | solution.py:208
  68.9 30.2 %shard_map.83 = bf16[2,12,96,2048]{3,2,1,0:T(8,128)(2,1)} custom-call(s32[12]{0:T(128)S(1)} %convert_reduce_fusion.offsets, bf16[2048,1024]{1,0:T(8,128)(2,1)} %constant.60.clone.basis, bf16[12,1024,192]{2,1,0:T(8,128)(2,1)} %shard_map.82.blocks, f32[64,24,384]{2,1,0:T(8,128)S(1)} %copy.46.rows), custom_call_target="tpu_custom_call" | custom-call | tf_op jit(solution)/shard_map/pallas_call | solution.py:123
  99.0 5.2 %dynamic-slice_bitcast_fusion = bf16[12,96,2048]{2,1,0:T(8,128)(2,1)} fusion(bf16[2,12,96,2048]{3,2,1,0:T(8,128)(2,1)} %shard_map.83, s32[]{:T(128)S(6)} %select_n.65), kind=kLoop, calls=%fused_computation.2 | loop fusion | bytes 9437188 | tf_op jit(solution)/shard_map/jit(dynamic_index_in_dim)/squeeze | solution.py:235
  104.2 8.2 %collective-permute-done.2 = bf16[12,96,2048]{2,1,0:T(8,128)(2,1)} collective-permute-done((bf16[12,96,2048]{2,1,0:T(8,128)(2,1)}, bf16[12,96,2048]{2,1,0:T(8,128)(2,1)}, u32[]{:S(2)}, u32[]{:S(2)}) %collective-permute-start.2) | collective-permute-done | bytes 4718624 | tf_op jit(solution)/shard_map/ppermute | solution.py:179
  112.4 6.0 %fusion = bf16[12,96,2048]{2,1,0:T(8,128)(2,1)S(1)} fusion(bf16[12,96,2048]{2,1,0:T(8,128)(2,1)} %collective-permute-done.2, bf16[2,12,96,2048]{3,2,1,0:T(8,128)(2,1)} %shard_map.83, s32[]{:T(128)S(6)} %select_n.64), kind=kLoop, calls=%fused_computation.1 | loop fusion | flops 9437184 | bytes 14155780 | tf_op jit(solution)/shard_map/convert_element_type | solution.py:236
  118.5 1.5 fusion.8
  120.0 1.1 copy-done
  121.0 1.3 collective-permute-start.4
  122.3 6.6 %collective-permute-start.3 = (bf16[4,96,2048]{2,1,0:T(8,128)(2,1)S(1)}, bf16[4,96,2048]{2,1,0:T(8,128)(2,1)}, u32[]{:S(2)}, u32[]{:S(2)}) collective-permute-start(bf16[4,96,2048]{2,1,0:T(8,128)(2,1)S(1)} %get-tuple-element.12), channel_id=1, source_target_pairs={{0,4},{4,8},{8,12},{12,16},{16,20},{20,24},{24,28},{1,5},{5,9},{9,... | collective-permute-start | bytes 4718600 | tf_op jit(solution)/shard_map/ppermute | solution.py:175
  129.0 31.7 %collective-permute-done.4 = bf16[4,96,2048]{2,1,0:T(8,128)(2,1)S(1)} collective-permute-done((bf16[4,96,2048]{2,1,0:T(8,128)(2,1)}, bf16[4,96,2048]{2,1,0:T(8,128)(2,1)S(1)}, u32[]{:S(2)}, u32[]{:S(2)}) %collective-permute-start.4) | collective-permute-done | bytes 1572896 | tf_op jit(solution)/shard_map/ppermute | solution.py:175
  160.8 33.9 %collective-permute-done.3 = bf16[4,96,2048]{2,1,0:T(8,128)(2,1)} collective-permute-done((bf16[4,96,2048]{2,1,0:T(8,128)(2,1)S(1)}, bf16[4,96,2048]{2,1,0:T(8,128)(2,1)}, u32[]{:S(2)}, u32[]{:S(2)}) %collective-permute-start.3) | collective-permute-done | bytes 1572896 | tf_op jit(solution)/shard_map/ppermute | solution.py:175
  194.6 2.2 broadcast_select_fusion.2
  196.8 1.6 collective-permute-start.5
  198.4 34.8 %collective-permute-done.5 = bf16[4,96,2048]{2,1,0:T(8,128)(2,1)S(1)} collective-permute-done((bf16[4,96,2048]{2,1,0:T(8,128)(2,1)S(1)}, bf16[4,96,2048]{2,1,0:T(8,128)(2,1)S(1)}, u32[]{:S(2)}, u32[]{:S(2)}) %collective-permute-start.5) | collective-permute-done | bytes 1572896 | tf_op jit(solution)/shard_map/ppermute | solution.py:179
  233.2 13.6 %shard_map.84 = f32[384,2048]{1,0:T(8,128)} custom-call(bf16[384,2048]{1,0:T(8,128)(2,1)S(1)} %bitcast.57, bf16[384,2048]{1,0:T(8,128)(2,1)S(1)} %bitcast.58, bf16[2048,2048]{1,0:T(8,128)(2,1)} %constant.61.clone.high, bf16[2048,2048]{1,0:T(8,128)(2,1)} %constant.62.clone.low), custom_call_target="tpu_custom_call" | custom-call | tf_op jit(solution)/shard_map/pallas_call | solution.py:157
  (35 shorter events, 3.2 us)
Async XLA Ops:
  0.0 23.6 %copy-start.2 = (s32[192]{0:T(256)S(1)}, s32[192]{0:T(256)}, u32[]{:S(2)}) copy-start(s32[192]{0:T(256)} %param.10) | copy-start | bytes 2308
  16.8 16.2 %collective-permute-start.1 = (bf16[4,12416]{1,0:T(4,128)(2,1)S(1)}, bf16[4,12416]{1,0:T(4,128)(2,1)S(1)}, u32[]{:S(2)}, u32[]{:S(2)}) collective-permute-start(bf16[4,12416]{1,0:T(4,128)(2,1)S(1)} %pad_maximum_fusion.3), channel_id=1, source_target_pairs={{4,0},{8,4},{12,8},{16,12},{20,16},{24,20},{28,24},{5,1},{9,5},{13... | collective-permute-start | bytes 297992 | tf_op jit(solution)/shard_map/ppermute | solution.py:175
  18.1 14.9 %collective-permute-start = (bf16[4,12416]{1,0:T(4,128)(2,1)S(1)}, bf16[4,12416]{1,0:T(4,128)(2,1)S(1)}, u32[]{:S(2)}, u32[]{:S(2)}) collective-permute-start(bf16[4,12416]{1,0:T(4,128)(2,1)S(1)} %pad_maximum_fusion.3), channel_id=1, source_target_pairs={{0,4},{4,8},{8,12},{12,16},{16,20},{20,24},{24,28},{1,5},{5,9},{9,... | collective-permute-start | bytes 297992 | tf_op jit(solution)/shard_map/ppermute | solution.py:175
  58.0 3.9 %copy-start.1 = (bf16[12,12,1,64,16]{3,4,2,1,0:T(8,128)(2,1)S(1)}, bf16[12,12,1,64,16]{3,4,2,1,0:T(8,128)(2,1)}, u32[]{:S(2)}) copy-start(bf16[12,12,1,64,16]{3,4,2,1,0:T(8,128)(2,1)} %copy.43) | copy-start | bytes 884740
  104.2 8.3 %collective-permute-start.2 = (bf16[12,96,2048]{2,1,0:T(8,128)(2,1)}, bf16[12,96,2048]{2,1,0:T(8,128)(2,1)}, u32[]{:S(2)}, u32[]{:S(2)}) collective-permute-start(bf16[12,96,2048]{2,1,0:T(8,128)(2,1)} %dynamic-slice_bitcast_fusion), channel_id=1, source_target_pairs={{0,1},{1,0},{2,3},{3,2},{4,5},{5,4},{6,7},{7,6},{8,9},{9,8},{10,11... | collective-permute-start | bytes 14155784 | tf_op jit(solution)/shard_map/ppermute | solution.py:179
  118.4 2.6 %copy-start = (bf16[12,96,2048]{2,1,0:T(8,128)(2,1)}, bf16[12,96,2048]{2,1,0:T(8,128)(2,1)S(1)}, u32[]{:S(2)}) copy-start(bf16[12,96,2048]{2,1,0:T(8,128)(2,1)S(1)} %fusion) | copy-start | bytes 14155780
  121.0 39.7 %collective-permute-start.4 = (bf16[4,96,2048]{2,1,0:T(8,128)(2,1)}, bf16[4,96,2048]{2,1,0:T(8,128)(2,1)S(1)}, u32[]{:S(2)}, u32[]{:S(2)}) collective-permute-start(bf16[4,96,2048]{2,1,0:T(8,128)(2,1)} %get-tuple-element.11), channel_id=1, source_target_pairs={{4,0},{8,4},{12,8},{16,12},{20,16},{24,20},{28,24},{5,1},{9,5},{13... | collective-permute-start | bytes 4718600 | tf_op jit(solution)/shard_map/ppermute | solution.py:175
  122.3 72.3 %collective-permute-start.3 = (bf16[4,96,2048]{2,1,0:T(8,128)(2,1)S(1)}, bf16[4,96,2048]{2,1,0:T(8,128)(2,1)}, u32[]{:S(2)}, u32[]{:S(2)}) collective-permute-start(bf16[4,96,2048]{2,1,0:T(8,128)(2,1)S(1)} %get-tuple-element.12), channel_id=1, source_target_pairs={{0,4},{4,8},{8,12},{12,16},{16,20},{20,24},{24,28},{1,5},{5,9},{9,... | collective-permute-start | bytes 4718600 | tf_op jit(solution)/shard_map/ppermute | solution.py:175
  196.8 36.4 %collective-permute-start.5 = (bf16[4,96,2048]{2,1,0:T(8,128)(2,1)S(1)}, bf16[4,96,2048]{2,1,0:T(8,128)(2,1)S(1)}, u32[]{:S(2)}, u32[]{:S(2)}) collective-permute-start(bf16[4,96,2048]{2,1,0:T(8,128)(2,1)S(1)} %get-tuple-element.9), channel_id=1, source_target_pairs={{0,2},{1,3},{2,0},{3,1},{4,6},{5,7},{6,4},{7,5},{8,10},{9,11},{10,... | collective-permute-start | bytes 4718600 | tf_op jit(solution)/shard_map/ppermute | solution.py:179

commit v2 on v1

--- a/solution.py
+++ b/solution.py
@@ -83,63 +83,96 @@
     )(samples, jnp.swapaxes(exponents, 0, 1), alive.astype(F32)[:, None])
 
 
-def cross_kernel(offsets, basis, blocks, rows, out, spec, weights, cross):
+def cross_kernel(offsets, basis, factors, blocks, sources, mine, other, spec, terms, weights, cross):
     seg_count, _, channels = blocks.shape
-    groups, terms, depth = rows.shape
-    sources = terms // 2
+    groups, depth, _ = spec.shape
+    count = mine.shape[0]
+    padded = sources.shape[0] // seg_count
+    width = groups * 2 * GROUP
     for n in range(seg_count):
         part = jnp.dot(basis[...], blocks[n], preferred_element_type=F32).astype(BF16)
         for q in range(groups):
             spec[q, n * 2 * GROUP : (n + 1) * 2 * GROUP, :] = part[q * 2 * GROUP : (q + 1) * 2 * GROUP]
+    terms[...] = (
+        jnp.dot(sources[...], factors[0], preferred_element_type=F32).astype(BF16).astype(F32)
+    )
     lane_bin = lax.broadcasted_iota(jnp.int32, (GROUP, depth), 1) % GROUP
     same = lane_bin == lax.broadcasted_iota(jnp.int32, (GROUP, depth), 0)
     for q in range(groups):
-        for s in range(terms):
-            row = jnp.broadcast_to(rows[q, s : s + 1, :], (GROUP, depth))
-            weights[q % 2, s * GROUP : (s + 1) * GROUP, :] = jnp.where(same, row, 0.0).astype(BF16)
+        for c in range(2):
+            at = c * width + q * 2 * GROUP
+            rows = jnp.concatenate(
+                [terms[n * padded : (n + 1) * padded, at : at + 2 * GROUP] for n in range(seg_count)], axis=1
+            )
+            for s in range(count):
+                row = jnp.broadcast_to(rows[s : s + 1, :], (GROUP, depth))
+                start = (2 * s + c) * GROUP
+                weights[q % 2, start : start + GROUP, :] = jnp.where(same, row, 0.0).astype(BF16)
         product = jnp.dot(weights[q % 2], spec[q], preferred_element_type=F32).astype(BF16)
-        for s in range(sources):
+        for s in range(count):
             cross[s, q * 2 * GROUP : (q + 1) * 2 * GROUP, :] = product[s * 2 * GROUP : (s + 1) * 2 * GROUP]
     target = lax.broadcasted_iota(jnp.int32, (channels, channels), 0)
     origin = lax.broadcasted_iota(jnp.int32, (channels, channels), 1)
     half = channels // 2
-    for s in range(sources):
+    for s in range(count):
         at = target + offsets[s]
         at = jnp.where(at >= channels, at - channels, at)
         turn = jnp.where(at == origin, 1.0, 0.0).astype(BF16)
         turned = lax.dot_general(
             turn, cross[s], (((1,), (1,)), ((), ())), preferred_element_type=F32
         ).astype(BF16)
-        out[0, s] = turned[:half]
-        out[1, s] = turned[half:]
-
-
-def cross_terms(offsets, blocks, rows, first, count):
+        mine[s] = turned[:half]
+        other[s] = turned[half:]
+
+
+STEP = 8
+
+
+@functools.lru_cache(None)
+def factor_table():
+    basis = forward_basis()
+    real, imag = basis[:, :SEG], basis[:, SEG:]
+    order = bin_order()
+    straight = basis[:, order].reshape(SEG, -1, STEP * 2 * GROUP)
+    crossed = np.concatenate([-imag, real], axis=1)[:, order].reshape(SEG, -1, STEP * 2 * GROUP)
+    return np.ascontiguousarray(np.concatenate([straight, crossed], axis=2).transpose(1, 0, 2))
+
+
+def cross_terms(offsets, blocks, sources, first, steps):
     seg_count, _, channels = blocks.shape
-    _, terms, depth = rows.shape
-    step = 8
-    width = step * 2 * GROUP
-    basis = jnp.asarray(forward_basis().T[bin_order()][first * 2 * GROUP : (first + count) * 2 * GROUP])
+    count = offsets.shape[0]
+    width = STEP * 2 * GROUP
+    depth = seg_count * 2 * GROUP
+    rows = forward_basis().T[bin_order()]
+    basis = jnp.asarray(np.ascontiguousarray(rows[first * width : (first + steps) * width]))
+    factors = jnp.asarray(factor_table()[first : first + steps])
+    half = jax.ShapeDtypeStruct((count, channels // 2, steps * width), BF16)
+    half_spec = pl.BlockSpec((count, channels // 2, width), lambda i, o: (0, 0, i))
     return pl.pallas_call(
         cross_kernel,
         grid_spec=pltpu.PrefetchScalarGridSpec(
             num_scalar_prefetch=1,
-            grid=(count // step,),
+            grid=(steps,),
             in_specs=[
                 pl.BlockSpec((width, SEG), lambda i, o: (i, 0)),
+                pl.BlockSpec((1, SEG, 2 * width), lambda i, o: (i, 0, 0)),
                 pl.BlockSpec((seg_count, SEG, channels), lambda i, o: (0, 0, 0)),
-                pl.BlockSpec((step, terms, depth), lambda i, o: (i + first // step, 0, 0)),
+                pl.BlockSpec(sources.shape, lambda i, o: (0, 0)),
             ],
-            out_specs=pl.BlockSpec((2, terms // 2, channels // 2, width), lambda i, o: (0, 0, 0, i)),
+            out_specs=[half_spec, half_spec],
             scratch_shapes=[
-                pltpu.VMEM((step, depth, channels), BF16),
-                pltpu.VMEM((2, terms * GROUP, depth), BF16),
-                pltpu.VMEM((terms // 2, width, channels), BF16),
+                pltpu.VMEM((STEP, depth, channels), BF16),
+                pltpu.VMEM((sources.shape[0], 2 * width), F32),
+                pltpu.VMEM((2, count * 2 * GROUP, depth), BF16),
+                pltpu.VMEM((count, width, channels), BF16),
             ],
         ),
-        out_shape=jax.ShapeDtypeStruct((2, terms // 2, channels // 2, count * 2 * GROUP), BF16),
+        out_shape=[half, half],
+        cost_estimate=pl.CostEstimate(
+            flops=steps * 4_500_000_000, bytes_accessed=steps * 4_000_000, transcendentals=0
+        ),
         compiler_params=pltpu.CompilerParams(vmem_limit_bytes=48 * 2**20),
-    )(offsets, basis, blocks, rows)
+    )(offsets, basis, factors, blocks, sources)
 
 
 def lag_kernel(kept, came, high, low, out):
@@ -195,57 +228,89 @@
     return jnp.concatenate([normed, tail], axis=1)
 
 
-def source_terms(sources):
-    count, length = sources.shape
-    seg_count = length // SEG
-    spectra = jnp.dot(
-        sources.reshape(count * seg_count, SEG), jnp.asarray(forward_basis()), preferred_element_type=F32
-    ).astype(BF16)
-    spectra = spectra.reshape(count, seg_count, 2, SEG // GROUP, GROUP)
-    real, imag = spectra[:, :, 0], spectra[:, :, 1]
-    pair = jnp.stack([jnp.stack([real, imag], 2), jnp.stack([-imag, real], 2)], 1)
-    rows = jnp.transpose(pair, (4, 0, 1, 2, 3, 5))
-    return rows.reshape(SEG // GROUP, count * 2, seg_count * 2 * GROUP).astype(F32)
-
-
-CHUNKS = 1
+def chan_first(pair, low_part, side, here):
+    below = passed_along(pair[2 * here :], "chan", 1)
+    above = passed_along(pair[:here], "chan", -1)
+    yield below, above
+    below, above = yield
+    own = pair[here : 2 * here]
+    first = jnp.where(low_part, below, own)
+    second = jnp.where(low_part, own, above)
+    kept = jnp.where(side == 0, first, second)
+    yield kept, swapped(jnp.where(side == 0, second, first), 2)
+
+
+def side_first(pair, low_part, side, here):
+    lower, upper = pair[: 2 * here], pair[here:]
+    came = swapped(jnp.where(side == 0, lower, upper), 2)
+    yield (came,)
+    (came,) = yield
+    own = pair[here : 2 * here]
+    outer = jnp.where(side == 0, pair[2 * here :], pair[:here])
+    came_own = jnp.where(side == 0, came[:here], came[here:])
+    came_outer = jnp.where(side == 0, came[here:], came[:here])
+    outer = (outer.astype(F32) + came_outer.astype(F32)).astype(BF16)
+    chans, wins = lax.axis_size("chan"), lax.axis_size("win")
+    route = [
+        (d * wins + w, e * wins + w)
+        for d in range(chans)
+        for w in range(wins)
+        for e in [d + 1 if w // 2 == 0 else d - 1]
+        if 0 <= e < chans
+    ]
+    came_over = lax.ppermute(outer, ("chan", "win"), route)
+    over = low_part == (side == 0)
+    yield jnp.where(over, came_over, own), jnp.where(over, jnp.zeros_like(own), came_own)
+
+
+PLAN = (chan_first, side_first, chan_first, side_first)
 
 
 def shards(samples, exponents, alive, offsets):
     channels, windows, length = samples.shape
-    per_device = offsets.shape[0]
+    here = offsets.shape[0]
     win = lax.axis_index("win")
     core, side = win % 2, win // 2
+    half = channels // 2
+    seg_count = windows * length // SEG
     own = source_rows(samples, exponents, alive, offsets)
     sources = jnp.concatenate(
         [passed_along(own, "chan", 1), own, passed_along(own, "chan", -1)], axis=0
     )
-    places = sources[:, windows * length].astype(jnp.int32)
-    rows = source_terms(sources[:, : windows * length])
+    places = sources[:, windows * length].astype(jnp.int32) + core * half
+    places = jnp.where(places >= channels, places - channels, places)
+    count = places.shape[0]
+    sources = jnp.swapaxes(sources[:, : windows * length].reshape(count, seg_count, SEG), 0, 1)
+    sources = jnp.pad(sources, ((0, 0), (0, -count % 16), (0, 0))).reshape(-1, SEG)
     blocks = normalize_blocks(samples, exponents, alive)
-    half = channels // 2
     turned = (core * half + jnp.arange(half, dtype=jnp.int32))[None, :, None]
     low_part = turned < (channels - offsets)[:, None, None]
     kept, came = [], []
-    groups = SEG // GROUP
-    count = groups // CHUNKS
-    for c in range(CHUNKS):
-        terms = cross_terms(places, blocks, rows, c * count, count)
-        mine = lax.dynamic_index_in_dim(terms, core, 0, keepdims=False)
-        other = swapped(lax.dynamic_index_in_dim(terms, 1 - core, 0, keepdims=False), 1)
-        pair = (mine.astype(F32) + other.astype(F32)).astype(BF16)
-        below = passed_along(pair[2 * per_device :], "chan", 1)
-        above = passed_along(pair[:per_device], "chan", -1)
-        here = pair[per_device : 2 * per_device]
-        first = jnp.where(low_part, below, here)
-        second = jnp.where(low_part, here, above)
-        kept.append(jnp.where(side == 0, first, second))
-        came.append(swapped(jnp.where(side == 0, second, first), 2))
-    kept = jnp.concatenate(kept, axis=-1).reshape(per_device * half, 2 * SEG)
-    came = jnp.concatenate(came, axis=-1).reshape(per_device * half, 2 * SEG)
+    steps = SEG // GROUP // STEP // len(PLAN)
+    pairs, ways, hops = [], [], []
+    for c in range(len(PLAN)):
+        if c >= 2:
+            places, pairs[c - 2] = lax.optimization_barrier((places, pairs[c - 2]))
+            ways.append(PLAN[c - 2](pairs[c - 2], low_part, side, here))
+            hops.append(next(ways[-1]))
+        if c >= 3:
+            places, hops[c - 3] = lax.optimization_barrier((places, hops[c - 3]))
+        mine, other = cross_terms(places, blocks, sources, c * steps, steps)
+        places, other = lax.optimization_barrier((places, other))
+        pairs.append((mine.astype(F32) + swapped(other, 1).astype(F32)).astype(BF16))
+    for c in range(len(PLAN)):
+        if c >= len(ways):
+            ways.append(PLAN[c](pairs[c], low_part, side, here))
+            hops.append(next(ways[-1]))
+        next(ways[c])
+        a, b = ways[c].send(hops[c])
+        kept.append(a)
+        came.append(b)
+    kept = jnp.concatenate(kept, axis=-1).reshape(here * half, 2 * SEG)
+    came = jnp.concatenate(came, axis=-1).reshape(here * half, 2 * SEG)
     high, low = lag_tables(windows * lax.axis_size("win"), length // SEG)
     result = lag_product(kept, came, jnp.asarray(high), jnp.asarray(low))
-    return result.reshape(per_device, half, 2 * SEG)
+    return result.reshape(here, half, 2 * SEG)
 
 
 def solution(mesh):

time: 248 us -> 192 us (0.77)
  waiting for transfers between devices: 109 us -> 48.7 us
  local copies, waits for them, and re-layouts: 41.6 us -> 8.6 us
  starting transfers between devices: 16.3 us -> 42.5 us
  Pallas kernels: 53 us -> 68.9 us
  matrix products: 2.98 us -> 0 us
  other arithmetic: 16.6 us -> 13.8 us
    ppermute x4 -> x6, waiting for transfers between devices: 65.6 us -> 12.2 us  [passed_along(): return lax.ppermute(block, axis, route)]
    pallas_call x1 -> x4, Pallas kernels: 30.2 us -> 46.1 us  [cross_terms(): pl.pallas_call(cross_kernel, grid_spec=pltpu.PrefetchScalarGridSpec(num_s...]
    ppermute x2 -> x8, starting transfers between devices: 1.56 us -> 14 us  [swapped(): lax.ppermute(block, 'win', [(i, i ^ bit) for i in range(lax.axis_size('wi...]
    another operation x2 -> x0, local copies, waits for them, and re-layouts: 8.88 us -> none  [source_terms(): jnp.stack([jnp.stack([real, imag], 2), jnp.stack([-imag, real], 2)], 1)]
    ppermute x0 -> x2, starting transfers between devices: none -> 8.83 us  [side_first(): came_over = lax.ppermute(outer, ('chan', 'win'), route)]
    slice x3 -> x2, local copies, waits for them, and re-layouts: 8.59 us -> 0.13 us  [chan_first(): above = passed_along(pair[:here], 'chan', -1)]
    ppermute x2 -> x8, waiting for transfers between devices: 43.1 us -> 36.5 us  [swapped(): lax.ppermute(block, 'win', [(i, i ^ bit) for i in range(lax.axis_size('wi...]
    squeeze x1 -> x0, local copies, waits for them, and re-layouts: 5.17 us -> none  [shards(): lax.dynamic_index_in_dim(terms, 1 - core, 0, keepdims=False)]
  transfers between devices with their start and end apart: 6 -> 16, of which waited for: 4 -> 7; matrix products, arithmetic and copies ran while one was open for 0% -> 4% of each run, Pallas kernels for 4% -> 17%
where the time goes in v2:
time: 192 us; the launch traced here: 191 us
  Pallas kernels  68.9 us (36%)
  waiting for transfers between devices  48.7 us (25%)
  starting transfers between devices  42.5 us (22%)
  other arithmetic  13.8 us (7%)
  local copies, waits for them, and re-layouts  8.6 us (4%)
  between operations  8.15 us (4%)
    pallas_call x4, Pallas kernels, cross_terms(): pl.pallas_call(cross_kernel, grid_spec=pltpu.PrefetchScalarGridSpec(num_s...  46.1 us
    ppermute x8, waiting for transfers between devices, swapped(): lax.ppermute(block, 'win', [(i, i ^ bit) for i in range(lax.axis_size('wi...  36.5 us
    ppermute x6, starting transfers between devices, passed_along(): return lax.ppermute(block, axis, route)  19.7 us
    ppermute x8, starting transfers between devices, swapped(): lax.ppermute(block, 'win', [(i, i ^ bit) for i in range(lax.axis_size('wi...  14 us
    pallas_call x1, Pallas kernels, lag_product(): pl.pallas_call(lag_kernel, grid=(2 * SEG // width,), in_specs=[pl.BlockSp...  13.6 us
    ppermute x6, waiting for transfers between devices, passed_along(): return lax.ppermute(block, axis, route)  12.2 us
    pallas_call x1, Pallas kernels, normalize_blocks(): pl.pallas_call(norm_kernel, out_shape=jax.ShapeDtypeStruct((windows * len...  9.23 us
    ppermute x2, starting transfers between devices, side_first(): came_over = lax.ppermute(outer, ('chan', 'win'), route)  8.83 us
  transfers between devices with their start and end apart: 16, of which 7 were waited for; matrix products, arithmetic and copies ran while one was open for 4% of the time, Pallas kernels for 17%

profile of v2, /device:TPU:0, one launch (start us, length us, event | category | flops | bytes accessed | tf_op | source)
XLA Modules:
  0.0 190.7 jit_solution(2509749119679617053)
XLA Ops:
  0.0 1.5 fusion.10
  6.5 1.3 broadcast_subtract_fusion
  12.1 1.5 fusion.9
  13.7 2.6 %add_convert_fusion.8 = f32[4]{0:T(128)S(1)} fusion(s32[1]{0:T(128)} %get-tuple-element.70, s32[1]{0:T(128)} %get-tuple-element.68, s32[1]{0:T(128)} %get-tuple-element.69, s32[1]{0:T(128)} %get-tuple-element.67), kind=kLoop, calls=%fused_computation.55 | loop fusion | flops 16 | bytes 32 | tf_op jit(solution)/shard_map/convert_element_type | solution.py:225
  17.6 4.9 %collective-permute-start = (bf16[4,12416]{1,0:T(4,128)(2,1)S(1)}, bf16[4,12416]{1,0:T(4,128)(2,1)S(1)}, u32[]{:S(2)}, u32[]{:S(2)}) collective-permute-start(bf16[4,12416]{1,0:T(4,128)(2,1)S(1)} %pad_maximum_fusion.5), channel_id=1, source_target_pairs={{0,4},{4,8},{8,12},{12,16},{16,20},{20,24},{24,28},{1,5},{5,9},{9,... | collective-permute-start | bytes 297992 | tf_op jit(solution)/shard_map/ppermute | solution.py:208
  22.4 1.3 collective-permute-start.1
  23.9 9.2 %shard_map.136.blocks = bf16[12,1024,192]{2,1,0:T(8,128)(2,1)} custom-call(s32[192,2,6144]{2,1,0:T(2,128)} %samples.1, s32[2,192,24]{2,1,0:T(8,128)S(1)} %bitcast.49, f32[192,1]{1,0:T(8,128)S(1)} %copy.31.alive), custom_call_target="tpu_custom_call" | custom-call | tf_op jit(solution)/shard_map/pallas_call | solution.py:69
  35.4 1.3 reshape.184
  37.8 11.5 %shard_map.137 = (bf16[12,96,512]{2,1,0:T(8,128)(2,1)S(1)}, bf16[12,96,512]{2,1,0:T(8,128)(2,1)S(1)}) custom-call(s32[12]{0:T(128)S(1)} %compare_select_fusion.offsets, bf16[512,1024]{1,0:T(8,128)(2,1)S(1)} %copy-done.7, bf16[2,1024,512]{2,1,0:T(8,128)(2,1)S(1)} %copy-done.3, bf16[12,1024,192]{2,1,0:T(8,128)(2,1)} %shard_map.136.blocks, ...), custom_call_target="tpu_custom_call" | custom-call | flops 8999999488 | bytes 8000000 | tf_op jit(solution)/shard_map/pallas_call | solution.py:151
  49.4 11.3 %shard_map.138 = (bf16[12,96,512]{2,1,0:T(8,128)(2,1)S(1)}, bf16[12,96,512]{2,1,0:T(8,128)(2,1)S(1)}) custom-call(s32[12]{0:T(128)S(1)} %compare_select_fusion.offsets, bf16[512,1024]{1,0:T(8,128)(2,1)S(1)} %copy-done.6, bf16[2,1024,512]{2,1,0:T(8,128)(2,1)S(1)} %copy-done.2, bf16[12,1024,192]{2,1,0:T(8,128)(2,1)} %shard_map.136.blocks, ...), custom_call_target="tpu_custom_call" | custom-call | flops 8999999488 | bytes 8000000 | tf_op jit(solution)/shard_map/pallas_call | solution.py:151
  61.7 4.8 %collective-permute-start.4 = (bf16[4,96,512]{2,1,0:T(8,128)(2,1)S(1)}, bf16[4,96,512]{2,1,0:T(8,128)(2,1)S(1)}, u32[]{:S(2)}, u32[]{:S(2)}) collective-permute-start(bf16[4,96,512]{2,1,0:T(8,128)(2,1)S(1)} %get-tuple-element.62), channel_id=1, source_target_pairs={{0,4},{4,8},{8,12},{12,16},{16,20},{20,24},{24,28},{1,5},{5,9},{9,... | collective-permute-start | bytes 1179656 | tf_op jit(solution)/shard_map/ppermute | solution.py:208
  66.5 1.5 collective-permute-start.5
  68.0 11.3 %shard_map.139 = (bf16[12,96,512]{2,1,0:T(8,128)(2,1)S(1)}, bf16[12,96,512]{2,1,0:T(8,128)(2,1)S(1)}) custom-call(s32[12]{0:T(128)S(1)} %compare_select_fusion.offsets, bf16[512,1024]{1,0:T(8,128)(2,1)S(1)} %copy-done.5, bf16[2,1024,512]{2,1,0:T(8,128)(2,1)S(1)} %copy-done.1, bf16[12,1024,192]{2,1,0:T(8,128)(2,1)} %shard_map.136.blocks, ...), custom_call_target="tpu_custom_call" | custom-call | flops 8999999488 | bytes 8000000 | tf_op jit(solution)/shard_map/pallas_call | solution.py:151
  79.4 1.4 add_convert_fusion.2
  80.8 2.7 %collective-permute-done.4 = bf16[4,96,512]{2,1,0:T(8,128)(2,1)S(1)} collective-permute-done((bf16[4,96,512]{2,1,0:T(8,128)(2,1)S(1)}, bf16[4,96,512]{2,1,0:T(8,128)(2,1)S(1)}, u32[]{:S(2)}, u32[]{:S(2)}) %collective-permute-start.4) | collective-permute-done | bytes 393248 | tf_op jit(solution)/shard_map/ppermute | solution.py:208
  83.5 12.1 %shard_map.140 = (bf16[12,96,512]{2,1,0:T(8,128)(2,1)S(1)}, bf16[12,96,512]{2,1,0:T(8,128)(2,1)}) custom-call(s32[12]{0:T(128)S(1)} %compare_select_fusion.offsets, bf16[512,1024]{1,0:T(8,128)(2,1)S(1)} %copy-done.4, bf16[2,1024,512]{2,1,0:T(8,128)(2,1)S(1)} %copy-done, bf16[12,1024,192]{2,1,0:T(8,128)(2,1)} %shard_map.136.blocks, bf16[192,1024]{1,0:T(8,128)(2,1)S(1)} %bitcast.53), custom_call_target="tpu_custom_call" | custom-call | flops 8999999488 | bytes 8000000 | tf_op jit(solution)/shard_map/pallas_call | solution.py:151
  96.1 1.5 slice_select_fusion.1
  97.5 1.6 collective-permute-start.6
  99.5 1.6 add_convert_fusion
  101.3 1.6 collective-permute-start.12
  102.8 15.2 %collective-permute-done.6 = bf16[8,96,512]{2,1,0:T(8,128)(2,1)S(1)} collective-permute-done((bf16[8,96,512]{2,1,0:T(8,128)(2,1)S(1)}, bf16[8,96,512]{2,1,0:T(8,128)(2,1)S(1)}, u32[]{:S(2)}, u32[]{:S(2)}) %collective-permute-start.6) | collective-permute-done | bytes 786464 | tf_op jit(solution)/shard_map/ppermute | solution.py:212
  118.2 4.4 %collective-permute-start.7 = (bf16[4,96,512]{2,1,0:T(8,128)(2,1)S(1)}, bf16[4,96,512]{2,1,0:T(8,128)(2,1)S(1)}, u32[]{:S(2)}, u32[]{:S(2)}) collective-permute-start(bf16[4,96,512]{2,1,0:T(8,128)(2,1)S(1)} %add_convert_fusion.5), channel_id=1, source_target_pairs={{0,4},{1,5},{4,8},{5,9},{6,2},{7,3},{8,12},{9,13},{10,6},{11,7},{1... | collective-permute-start | bytes 1179656 | tf_op jit(solution)/shard_map/ppermute | solution.py:261
  123.1 1.4 collective-permute-start.10
  124.5 5.8 %collective-permute-start.9 = (bf16[4,96,512]{2,1,0:T(8,128)(2,1)S(1)}, bf16[4,96,512]{2,1,0:T(8,128)(2,1)S(1)}, u32[]{:S(2)}, u32[]{:S(2)}) collective-permute-start(bf16[4,96,512]{2,1,0:T(8,128)(2,1)S(1)} %get-tuple-element.60), channel_id=1, source_target_pairs={{0,4},{4,8},{8,12},{12,16},{16,20},{20,24},{24,28},{1,5},{5,9},{9,... | collective-permute-start | bytes 1179656 | tf_op jit(solution)/shard_map/ppermute | solution.py:208
  130.4 3.6 %collective-permute-done.12 = bf16[8,96,512]{2,1,0:T(8,128)(2,1)S(1)} collective-permute-done((bf16[8,96,512]{2,1,0:T(8,128)(2,1)S(1)}, bf16[8,96,512]{2,1,0:T(8,128)(2,1)S(1)}, u32[]{:S(2)}, u32[]{:S(2)}) %collective-permute-start.12) | collective-permute-done | bytes 786464 | tf_op jit(solution)/shard_map/ppermute | solution.py:212
  134.2 4.4 %collective-permute-start.13 = (bf16[4,96,512]{2,1,0:T(8,128)(2,1)S(1)}, bf16[4,96,512]{2,1,0:T(8,128)(2,1)S(1)}, u32[]{:S(2)}, u32[]{:S(2)}) collective-permute-start(bf16[4,96,512]{2,1,0:T(8,128)(2,1)S(1)} %add_convert_fusion.4), channel_id=1, source_target_pairs={{0,4},{1,5},{4,8},{5,9},{6,2},{7,3},{8,12},{9,13},{10,6},{11,7},{1... | collective-permute-start | bytes 1179656 | tf_op jit(solution)/shard_map/ppermute | solution.py:261
  138.7 9.5 %collective-permute-done.9 = bf16[4,96,512]{2,1,0:T(8,128)(2,1)S(1)} collective-permute-done((bf16[4,96,512]{2,1,0:T(8,128)(2,1)S(1)}, bf16[4,96,512]{2,1,0:T(8,128)(2,1)S(1)}, u32[]{:S(2)}, u32[]{:S(2)}) %collective-permute-start.9) | collective-permute-done | bytes 393248 | tf_op jit(solution)/shard_map/ppermute | solution.py:208
  148.2 1.2 broadcast_select_fusion.4
  149.5 9.7 %collective-permute-start.14 = (bf16[4,96,512]{2,1,0:T(8,128)(2,1)S(1)}, bf16[4,96,512]{2,1,0:T(8,128)(2,1)S(1)}, u32[]{:S(2)}, u32[]{:S(2)}) collective-permute-start(bf16[4,96,512]{2,1,0:T(8,128)(2,1)S(1)} %get-tuple-element.55), channel_id=1, source_target_pairs={{0,2},{1,3},{2,0},{3,1},{4,6},{5,7},{6,4},{7,5},{8,10},{9,11},{10,... | collective-permute-start | bytes 1179656 | tf_op jit(solution)/shard_map/ppermute | solution.py:212
  159.7 9.4 %collective-permute-done.14 = bf16[4,96,512]{2,1,0:T(8,128)(2,1)S(1)} collective-permute-done((bf16[4,96,512]{2,1,0:T(8,128)(2,1)S(1)}, bf16[4,96,512]{2,1,0:T(8,128)(2,1)S(1)}, u32[]{:S(2)}, u32[]{:S(2)}) %collective-permute-start.14) | collective-permute-done | bytes 393248 | tf_op jit(solution)/shard_map/ppermute | solution.py:212
  169.1 7.8 %collective-permute-done.15 = bf16[4,96,512]{2,1,0:T(8,128)(2,1)S(1)} collective-permute-done((bf16[4,96,512]{2,1,0:T(8,128)(2,1)S(1)}, bf16[4,96,512]{2,1,0:T(8,128)(2,1)S(1)}, u32[]{:S(2)}, u32[]{:S(2)}) %collective-permute-start.15) | collective-permute-done | bytes 393248 | tf_op jit(solution)/shard_map/ppermute | solution.py:212
  177.1 13.6 %shard_map.141 = f32[384,2048]{1,0:T(8,128)} custom-call(bf16[384,2048]{1,0:T(8,128)(2,1)S(1)} %bitcast.47, bf16[384,2048]{1,0:T(8,128)(2,1)S(1)} %bitcast.48, bf16[2048,2048]{1,0:T(8,128)(2,1)} %constant.76.clone.high, bf16[2048,2048]{1,0:T(8,128)(2,1)} %constant.77.clone.low), custom_call_target="tpu_custom_call" | custom-call | tf_op jit(solution)/shard_map/pallas_call | solution.py:190
  (92 shorter events, 10.2 us)
Async XLA Ops:
  13.6 10.1 %copy-start.17 = (s32[192]{0:T(256)S(1)}, s32[192]{0:T(256)}, u32[]{:S(2)}) copy-start(s32[192]{0:T(256)} %param.16) | copy-start | bytes 2308
  17.4 15.8 %copy-start.10 = (bf16[4,12288]{1,0:T(4,128)(2,1)}, bf16[4,12288]{1,0:T(4,128)(2,1)S(1)}, u32[]{:S(2)}) copy-start(bf16[4,12288]{1,0:T(4,128)(2,1)S(1)} %fusion.2) | copy-start | bytes 294916
  17.6 15.6 %collective-permute-start = (bf16[4,12416]{1,0:T(4,128)(2,1)S(1)}, bf16[4,12416]{1,0:T(4,128)(2,1)S(1)}, u32[]{:S(2)}, u32[]{:S(2)}) collective-permute-start(bf16[4,12416]{1,0:T(4,128)(2,1)S(1)} %pad_maximum_fusion.5), channel_id=1, source_target_pairs={{0,4},{4,8},{8,12},{12,16},{16,20},{20,24},{24,28},{1,5},{5,9},{9,... | collective-permute-start | bytes 297992 | tf_op jit(solution)/shard_map/ppermute | solution.py:208
  22.4 10.7 %collective-permute-start.1 = (bf16[4,12416]{1,0:T(4,128)(2,1)S(1)}, bf16[4,12416]{1,0:T(4,128)(2,1)S(1)}, u32[]{:S(2)}, u32[]{:S(2)}) collective-permute-start(bf16[4,12416]{1,0:T(4,128)(2,1)S(1)} %pad_maximum_fusion.5), channel_id=1, source_target_pairs={{4,0},{8,4},{12,8},{16,12},{20,16},{24,20},{28,24},{5,1},{9,5},{13... | collective-permute-start | bytes 297992 | tf_op jit(solution)/shard_map/ppermute | solution.py:208
  33.1 4.6 %copy-start.3 = (bf16[2,1024,512]{2,1,0:T(8,128)(2,1)S(1)}, bf16[2,1024,512]{2,1,0:T(8,128)(2,1)}, u32[]{:S(2)}) copy-start(bf16[2,1024,512]{2,1,0:T(8,128)(2,1)} %constant.69.clone.factors) | copy-start | bytes 6291460
  33.2 4.6 %copy-start.7 = (bf16[512,1024]{1,0:T(8,128)(2,1)S(1)}, bf16[512,1024]{1,0:T(8,128)(2,1)}, u32[]{:S(2)}) copy-start(bf16[512,1024]{1,0:T(8,128)(2,1)} %constant.68.clone.basis) | copy-start | bytes 3145732
  37.7 11.6 %copy-start.2 = (bf16[2,1024,512]{2,1,0:T(8,128)(2,1)S(1)}, bf16[2,1024,512]{2,1,0:T(8,128)(2,1)}, u32[]{:S(2)}) copy-start(bf16[2,1024,512]{2,1,0:T(8,128)(2,1)} %constant.71.clone.factors) | copy-start | bytes 6291460
  37.8 11.6 %copy-start.6 = (bf16[512,1024]{1,0:T(8,128)(2,1)S(1)}, bf16[512,1024]{1,0:T(8,128)(2,1)}, u32[]{:S(2)}) copy-start(bf16[512,1024]{1,0:T(8,128)(2,1)} %constant.70.clone.basis) | copy-start | bytes 3145732
  49.3 11.9 %collective-permute-start.2 = (bf16[12,96,512]{2,1,0:T(8,128)(2,1)S(1)}, bf16[12,96,512]{2,1,0:T(8,128)(2,1)S(1)}, u32[]{:S(2)}, u32[]{:S(2)}) collective-permute-start(bf16[12,96,512]{2,1,0:T(8,128)(2,1)S(1)} %get-tuple-element.32), channel_id=1, source_target_pairs={{0,1},{1,0},{2,3},{3,2},{4,5},{5,4},{6,7},{7,6},{8,9},{9,8},{10,11... | collective-permute-start | bytes 3538952 | tf_op jit(solution)/shard_map/ppermute | solution.py:212
  60.6 18.7 %collective-permute-start.3 = (bf16[12,96,512]{2,1,0:T(8,128)(2,1)S(1)}, bf16[12,96,512]{2,1,0:T(8,128)(2,1)S(1)}, u32[]{:S(2)}, u32[]{:S(2)}) collective-permute-start(bf16[12,96,512]{2,1,0:T(8,128)(2,1)S(1)} %get-tuple-element.37), channel_id=1, source_target_pairs={{0,1},{1,0},{2,3},{3,2},{4,5},{5,4},{6,7},{7,6},{8,9},{9,8},{10,11... | collective-permute-start | bytes 3538952 | tf_op jit(solution)/shard_map/ppermute | solution.py:212
  61.2 6.8 %copy-start.1 = (bf16[2,1024,512]{2,1,0:T(8,128)(2,1)S(1)}, bf16[2,1024,512]{2,1,0:T(8,128)(2,1)}, u32[]{:S(2)}) copy-start(bf16[2,1024,512]{2,1,0:T(8,128)(2,1)} %constant.73.clone.factors) | copy-start | bytes 6291460
  61.6 5.0 %copy-start.9 = (bf16[12,96,512]{2,1,0:T(8,128)(2,1)}, bf16[12,96,512]{2,1,0:T(8,128)(2,1)S(1)}, u32[]{:S(2)}) copy-start(bf16[12,96,512]{2,1,0:T(8,128)(2,1)S(1)} %add_convert_fusion.3) | copy-start | bytes 3538948
  61.6 6.4 %copy-start.5 = (bf16[512,1024]{1,0:T(8,128)(2,1)S(1)}, bf16[512,1024]{1,0:T(8,128)(2,1)}, u32[]{:S(2)}) copy-start(bf16[512,1024]{1,0:T(8,128)(2,1)} %constant.72.clone.basis) | copy-start | bytes 3145732
  61.7 21.8 %collective-permute-start.4 = (bf16[4,96,512]{2,1,0:T(8,128)(2,1)S(1)}, bf16[4,96,512]{2,1,0:T(8,128)(2,1)S(1)}, u32[]{:S(2)}, u32[]{:S(2)}) collective-permute-start(bf16[4,96,512]{2,1,0:T(8,128)(2,1)S(1)} %get-tuple-element.62), channel_id=1, source_target_pairs={{0,4},{4,8},{8,12},{12,16},{16,20},{20,24},{24,28},{1,5},{5,9},{9,... | collective-permute-start | bytes 1179656 | tf_op jit(solution)/shard_map/ppermute | solution.py:208
  66.5 16.9 %collective-permute-start.5 = (bf16[4,96,512]{2,1,0:T(8,128)(2,1)S(1)}, bf16[4,96,512]{2,1,0:T(8,128)(2,1)S(1)}, u32[]{:S(2)}, u32[]{:S(2)}) collective-permute-start(bf16[4,96,512]{2,1,0:T(8,128)(2,1)S(1)} %get-tuple-element.61), channel_id=1, source_target_pairs={{4,0},{8,4},{12,8},{16,12},{20,16},{24,20},{28,24},{5,1},{9,5},{13... | collective-permute-start | bytes 1179656 | tf_op jit(solution)/shard_map/ppermute | solution.py:208
  79.3 4.2 %copy-start = (bf16[2,1024,512]{2,1,0:T(8,128)(2,1)S(1)}, bf16[2,1024,512]{2,1,0:T(8,128)(2,1)}, u32[]{:S(2)}) copy-start(bf16[2,1024,512]{2,1,0:T(8,128)(2,1)} %constant.75.clone.factors) | copy-start | bytes 6291460
  83.5 12.1 %copy-start.13 = (bf16[4,96,512]{2,1,0:T(8,128)(2,1)}, bf16[4,96,512]{2,1,0:T(8,128)(2,1)S(1)}, u32[]{:S(2)}) copy-start(bf16[4,96,512]{2,1,0:T(8,128)(2,1)S(1)} %collective-permute-done.4) | copy-start | bytes 1179652
  83.5 12.1 %copy-start.15 = (bf16[4,96,512]{2,1,0:T(8,128)(2,1)}, bf16[4,96,512]{2,1,0:T(8,128)(2,1)S(1)}, u32[]{:S(2)}) copy-start(bf16[4,96,512]{2,1,0:T(8,128)(2,1)S(1)} %collective-permute-done.5) | copy-start | bytes 1179652
  95.6 4.0 %collective-permute-start.11 = (bf16[12,96,512]{2,1,0:T(8,128)(2,1)}, bf16[12,96,512]{2,1,0:T(8,128)(2,1)}, u32[]{:S(2)}, u32[]{:S(2)}) collective-permute-start(bf16[12,96,512]{2,1,0:T(8,128)(2,1)} %get-tuple-element.48), channel_id=1, source_target_pairs={{0,1},{1,0},{2,3},{3,2},{4,5},{5,4},{6,7},{7,6},{8,9},{9,8},{10,11... | collective-permute-start | bytes 3538952 | tf_op jit(solution)/shard_map/ppermute | solution.py:212
  95.6 27.0 %collective-permute-start.8 = (bf16[12,96,512]{2,1,0:T(8,128)(2,1)S(1)}, bf16[12,96,512]{2,1,0:T(8,128)(2,1)S(1)}, u32[]{:S(2)}, u32[]{:S(2)}) collective-permute-start(bf16[12,96,512]{2,1,0:T(8,128)(2,1)S(1)} %get-tuple-element.44), channel_id=1, source_target_pairs={{0,1},{1,0},{2,3},{3,2},{4,5},{5,4},{6,7},{7,6},{8,9},{9,8},{10,11... | collective-permute-start | bytes 3538952 | tf_op jit(solution)/shard_map/ppermute | solution.py:212
  97.5 20.5 %collective-permute-start.6 = (bf16[8,96,512]{2,1,0:T(8,128)(2,1)S(1)}, bf16[8,96,512]{2,1,0:T(8,128)(2,1)S(1)}, u32[]{:S(2)}, u32[]{:S(2)}) collective-permute-start(bf16[8,96,512]{2,1,0:T(8,128)(2,1)S(1)} %slice_select_fusion.1), channel_id=1, source_target_pairs={{0,2},{1,3},{2,0},{3,1},{4,6},{5,7},{6,4},{7,5},{8,10},{9,11},{10,... | collective-permute-start | bytes 2359304 | tf_op jit(solution)/shard_map/ppermute | solution.py:212
  101.2 16.9 %copy-start.8 = (bf16[12,96,512]{2,1,0:T(8,128)(2,1)S(1)}, bf16[12,96,512]{2,1,0:T(8,128)(2,1)}, u32[]{:S(2)}) copy-start(bf16[12,96,512]{2,1,0:T(8,128)(2,1)} %add_convert_fusion.2) | copy-start | bytes 3538948
  101.3 32.7 %collective-permute-start.12 = (bf16[8,96,512]{2,1,0:T(8,128)(2,1)S(1)}, bf16[8,96,512]{2,1,0:T(8,128)(2,1)S(1)}, u32[]{:S(2)}, u32[]{:S(2)}) collective-permute-start(bf16[8,96,512]{2,1,0:T(8,128)(2,1)S(1)} %slice_select_fusion), channel_id=1, source_target_pairs={{0,2},{1,3},{2,0},{3,1},{4,6},{5,7},{6,4},{7,5},{8,10},{9,11},{10,... | collective-permute-start | bytes 2359304 | tf_op jit(solution)/shard_map/ppermute | solution.py:212
  118.2 41.0 %collective-permute-start.7 = (bf16[4,96,512]{2,1,0:T(8,128)(2,1)S(1)}, bf16[4,96,512]{2,1,0:T(8,128)(2,1)S(1)}, u32[]{:S(2)}, u32[]{:S(2)}) collective-permute-start(bf16[4,96,512]{2,1,0:T(8,128)(2,1)S(1)} %add_convert_fusion.5), channel_id=1, source_target_pairs={{0,4},{1,5},{4,8},{5,9},{6,2},{7,3},{8,12},{9,13},{10,6},{11,7},{1... | collective-permute-start | bytes 1179656 | tf_op jit(solution)/shard_map/ppermute | solution.py:261
  123.0 15.6 %copy-start.18 = (s32[4]{0:T(128)S(1)}, s32[4]{0:T(128)}, u32[]{:S(2)}) copy-start(s32[4]{0:T(128)} %get-tuple-element.77) | copy-start | bytes 52
  123.0 25.2 %copy-start.14 = (bf16[4,96,512]{2,1,0:T(8,128)(2,1)S(1)}, bf16[4,96,512]{2,1,0:T(8,128)(2,1)}, u32[]{:S(2)}) copy-start(bf16[4,96,512]{2,1,0:T(8,128)(2,1)} %copy-done.13) | copy-start | bytes 1179652
  123.0 25.2 %copy-start.16 = (bf16[4,96,512]{2,1,0:T(8,128)(2,1)S(1)}, bf16[4,96,512]{2,1,0:T(8,128)(2,1)}, u32[]{:S(2)}) copy-start(bf16[4,96,512]{2,1,0:T(8,128)(2,1)} %copy-done.15) | copy-start | bytes 1179652
  123.1 15.6 %collective-permute-start.10 = (bf16[4,96,512]{2,1,0:T(8,128)(2,1)S(1)}, bf16[4,96,512]{2,1,0:T(8,128)(2,1)S(1)}, u32[]{:S(2)}, u32[]{:S(2)}) collective-permute-start(bf16[4,96,512]{2,1,0:T(8,128)(2,1)S(1)} %get-tuple-element.59), channel_id=1, source_target_pairs={{4,0},{8,4},{12,8},{16,12},{20,16},{24,20},{28,24},{5,1},{9,5},{13... | collective-permute-start | bytes 1179656 | tf_op jit(solution)/shard_map/ppermute | solution.py:208
  124.5 23.7 %collective-permute-start.9 = (bf16[4,96,512]{2,1,0:T(8,128)(2,1)S(1)}, bf16[4,96,512]{2,1,0:T(8,128)(2,1)S(1)}, u32[]{:S(2)}, u32[]{:S(2)}) collective-permute-start(bf16[4,96,512]{2,1,0:T(8,128)(2,1)S(1)} %get-tuple-element.60), channel_id=1, source_target_pairs={{0,4},{4,8},{8,12},{12,16},{16,20},{20,24},{24,28},{1,5},{5,9},{9,... | collective-permute-start | bytes 1179656 | tf_op jit(solution)/shard_map/ppermute | solution.py:208
  134.2 25.0 %collective-permute-start.13 = (bf16[4,96,512]{2,1,0:T(8,128)(2,1)S(1)}, bf16[4,96,512]{2,1,0:T(8,128)(2,1)S(1)}, u32[]{:S(2)}, u32[]{:S(2)}) collective-permute-start(bf16[4,96,512]{2,1,0:T(8,128)(2,1)S(1)} %add_convert_fusion.4), channel_id=1, source_target_pairs={{0,4},{1,5},{4,8},{5,9},{6,2},{7,3},{8,12},{9,13},{10,6},{11,7},{1... | collective-permute-start | bytes 1179656 | tf_op jit(solution)/shard_map/ppermute | solution.py:261
  149.5 19.6 %collective-permute-start.14 = (bf16[4,96,512]{2,1,0:T(8,128)(2,1)S(1)}, bf16[4,96,512]{2,1,0:T(8,128)(2,1)S(1)}, u32[]{:S(2)}, u32[]{:S(2)}) collective-permute-start(bf16[4,96,512]{2,1,0:T(8,128)(2,1)S(1)} %get-tuple-element.55), channel_id=1, source_target_pairs={{0,2},{1,3},{2,0},{3,1},{4,6},{5,7},{6,4},{7,5},{8,10},{9,11},{10,... | collective-permute-start | bytes 1179656 | tf_op jit(solution)/shard_map/ppermute | solution.py:212
  159.2 17.7 %collective-permute-start.15 = (bf16[4,96,512]{2,1,0:T(8,128)(2,1)S(1)}, bf16[4,96,512]{2,1,0:T(8,128)(2,1)S(1)}, u32[]{:S(2)}, u32[]{:S(2)}) collective-permute-start(bf16[4,96,512]{2,1,0:T(8,128)(2,1)S(1)} %get-tuple-element.72), channel_id=1, source_target_pairs={{0,2},{1,3},{2,0},{3,1},{4,6},{5,7},{6,4},{7,5},{8,10},{9,11},{10,... | collective-permute-start | bytes 1179656 | tf_op jit(solution)/shard_map/ppermute | solution.py:212
  (3 other events, 5.4 us)
